TPU v7x, 32 devices: a whole 2x2x4 slice. The times are simulated.
32 devices in a mesh: groups: 2 (over x), expert: 16 (over z, y, core).
Axes of the slice: x: 2, y: 2, z: 4, core: 2. Of those that a mesh axis runs over, the one named last changes fastest.
Arguments:
- tokens: bfloat16 [256, 7168], P(('groups', 'expert')), parts along dimension 0, may hold values from -6 to 6
- routes: int32 [256, 8], P(('groups', 'expert')), parts along dimension 0, may hold values from 0 to 15, all different within a row; in each aligned block of 8 rows (0 to 7, 8 to 15, ...) at most 6 rows name the same one
- gate_scale: float32 [256, 8], P(('groups', 'expert')), parts along dimension 0, may hold values from 0.05 to 0.4
- w_gate: bfloat16 [16, 7168, 2048], P('expert'), may hold values from -0.0625 to 0.0625
- w_up: bfloat16 [16, 7168, 2048], P('expert'), may hold values from -0.0625 to 0.0625
- w_down: bfloat16 [16, 2048, 7168], P('expert'), may hold values from -0.125 to 0.125
Outputs:
- mixed: bfloat16 [256, 7168], P(('groups', 'expert')), parts along dimension 0
There are 2 independent parts, one for each index of `groups`. A program takes and returns all parts, laid end to end along the dimension named above; an argument that names none is the same for every part. Nothing has to cross between parts.
Inputs may be any that keep to these rules, and one draw needn't show every extreme that they name: `routes`: each token names 8 different experts. Among the tokens of one device no expert is named by more than 6 tokens, a bound that some block reaches.
All inputs are finite; a program needn't handle non-finite values.
Results may differ from a plain program's by a relative error of at most 0.0085.
Values may be sent and summed in bfloat16 or wider, within the bound.
A program may use at most 192 MiB of HBM per device.

v0:
```python
import jax
import jax.numpy as jnp
from jax import lax
from jax.sharding import PartitionSpec as P

FF = 2048


def on_device(tokens, routes, gate_scale, w_gate, w_up, w_down):
    devices = lax.axis_size("expert")
    tok_count, top_count = routes.shape
    width = tokens.shape[1]
    slices = FF // w_gate.shape[2]
    experts = devices // slices
    capacity = tok_count * top_count // experts + 2
    flat = routes.reshape(-1)
    onehot = (flat[:, None] == jnp.arange(experts, dtype=jnp.int32)[None, :]).astype(jnp.int32)
    slot = jnp.sum((jnp.cumsum(onehot, axis=0) - onehot) * onehot, axis=1)
    position = flat * capacity + slot
    picks = position[:, None] == jnp.arange(experts * capacity, dtype=jnp.int32)[None, :]
    picks = picks.reshape(tok_count, top_count, experts * capacity)
    select = jnp.any(picks, axis=1).astype(jnp.bfloat16)
    buffer = lax.dot_general(
        select, tokens, (((0,), (0,)), ((), ())), preferred_element_type=jnp.float32
    ).astype(jnp.bfloat16)
    outgoing = jnp.broadcast_to(
        buffer.reshape(experts, 1, capacity, width), (experts, slices, capacity, width)
    )
    outgoing = outgoing.reshape(devices, capacity, width)
    arrived = lax.all_to_all(outgoing, "expert", split_axis=0, concat_axis=0, tiled=True)
    count = arrived.shape[1]
    flat_rows = arrived.reshape(-1, width)
    gate = jnp.dot(flat_rows, w_gate[0], preferred_element_type=jnp.float32)
    upper = jnp.dot(flat_rows, w_up[0], preferred_element_type=jnp.float32)
    hidden = (jax.nn.silu(gate) * upper).astype(jnp.bfloat16)
    result = jnp.dot(hidden, w_down[0], preferred_element_type=jnp.float32).astype(jnp.bfloat16)
    back = lax.all_to_all(
        result.reshape(devices, count, width), "expert", split_axis=0, concat_axis=0, tiled=True
    )
    summed = back.reshape(experts, slices, capacity, width).astype(jnp.float32).sum(axis=1)
    summed = summed.reshape(experts * capacity, width)
    weights = jnp.sum(picks.astype(jnp.float32) * gate_scale[:, :, None], axis=1)
    mixed = jnp.dot(
        weights, summed, precision=lax.Precision.HIGHEST, preferred_element_type=jnp.float32
    )
    return mixed.astype(jnp.bfloat16)


def solution(mesh):
    return jax.shard_map(
        on_device,
        mesh=mesh,
        in_specs=(
            P(("groups", "expert"), None),
            P(("groups", "expert"), None),
            P(("groups", "expert"), None),
            P("expert", None, None),
            P("expert", None, None),
            P("expert", None, None),
        ),
        out_specs=P(("groups", "expert"), None),
        check_vma=False,
    )
```

profile of v0, /device:TPU:15, one launch (start us, length us, event | category | flops | bytes accessed | tf_op | source)
XLA Modules:
  0.0 137.1 jit_solution(6258925025957875306)
XLA Ops:
  0.0 0.0 copy-start
  0.0 0.8 eq.29
  0.8 0.1 fusion.24
  0.9 0.1 reduce_window_sum.11
  1.0 0.2 select_reduce_fusion.1
  1.2 0.1 reduce_sum.25
  1.2 0.7 multiply_add_fusion
  1.9 0.1 fusion.23
  2.0 0.0 copy-done
  2.0 0.6 convolution_convert_fusion
  2.6 0.5 reshape_reshape.3
  3.2 48.1 %all_to_all.10 = bf16[16,6,7168]{2,1,0:T(8,128)(2,1)} all-to-all(bf16[16,6,7168]{2,1,0:T(8,128)(2,1)S(1)} %reshape_reshape.3), channel_id=1, replica_groups=mesh['groups'=2,'expert'=16] {'expert'}, dimensions={0} | all-to-all | bytes 2752512 | tf_op jit(solution)/shard_map/all_to_all | solution.py:30
  51.3 1.7 %reshape.33 = bf16[96,7168]{1,0:T(8,128)(2,1)S(1)} reshape(bf16[16,6,7168]{2,1,0:T(8,128)(2,1)} %all_to_all.10) | data formatting | bytes 2752512 | tf_op jit(solution)/shard_map/reshape | solution.py:32
  53.0 12.7 %fusion.4 = f32[96,2048]{1,0:T(8,128)} fusion(bf16[96,7168]{1,0:T(8,128)(2,1)S(1)} %reshape.33, bf16[1,7168,2048]{2,1,0:T(8,128)(2,1)} %param.9), kind=kOutput, calls=%fused_computation.4 | convolution fusion | flops 2818572288 | bytes 31522816 | tf_op jit(solution)/shard_map/dot_general | solution.py:33
  65.7 21.0 %fusion.6 = bf16[96,7168]{1,0:T(8,128)(2,1)S(1)} fusion(bf16[1,2048,7168]{2,1,0:T(8,128)(2,1)} %param.11, bf16[96,7168]{1,0:T(8,128)(2,1)S(1)} %reshape.33, bf16[1,7168,2048]{2,1,0:T(8,128)(2,1)} %param.10, f32[96,2048]{1,0:T(8,128)} %fusion.4), kind=kOutput, calls=%fused_computation.7 | convolution fusion | flops 5639012352 | bytes 62259200 | tf_op jit(solution)/shard_map/dot_general | solution.py:36
  86.7 1.5 %reshape.34 = bf16[16,6,7168]{2,1,0:T(8,128)(2,1)} reshape(bf16[96,7168]{1,0:T(8,128)(2,1)S(1)} %fusion.6) | data formatting | bytes 2752512 | tf_op jit(solution)/shard_map/reshape | solution.py:38
  88.3 5.2 %all-to-all-start.1 = ((bf16[16,6,7168]{2,1,0:T(8,128)(2,1)}), bf16[16,6,7168]{2,1,0:T(8,128)(2,1)S(1)}, u32[]{:S(2)}, u32[]{:S(2)}) async-start(bf16[16,6,7168]{2,1,0:T(8,128)(2,1)} %reshape.34), calls=%async_computation.1 | async-start | bytes 3670016 | tf_op jit(solution)/shard_map/all_to_all | solution.py:37
  93.5 0.0 copy-done.2
  93.5 0.0 copy-start.1
  93.5 0.1 select_reduce_fusion
  93.6 41.7 %all-to-all-done.1 = bf16[16,6,7168]{2,1,0:T(8,128)(2,1)S(1)} async-done(((bf16[16,6,7168]{2,1,0:T(8,128)(2,1)}), bf16[16,6,7168]{2,1,0:T(8,128)(2,1)S(1)}, u32[]{:S(2)}, u32[]{:S(2)}) %all-to-all-start.1) | async-done | bytes 1376288 | tf_op jit(solution)/shard_map/all_to_all | solution.py:37
  135.3 0.5 reshape.35
  135.8 1.3 convolution_convert_fusion.1
  137.1 0.0 copy-done.1
  (1 shorter events, 0.0 us)
Async XLA Ops:
  0.0 2.0 %copy-start = (bf16[8,7168]{1,0:T(8,128)(2,1)S(1)}, bf16[8,7168]{1,0:T(8,128)(2,1)}, u32[]{:S(2)}) copy-start(bf16[8,7168]{1,0:T(8,128)(2,1)} %param.6) | copy-start | bytes 344068
  88.3 5.2 %copy-start.2 = (f32[8,8]{1,0:T(8,128)S(1)}, f32[8,8]{1,0:T(8,128)}, u32[]{:S(2)}) copy-start(f32[8,8]{1,0:T(8,128)} %param.8) | copy-start | bytes 772
  88.3 47.0 %all-to-all-start.1 = ((bf16[16,6,7168]{2,1,0:T(8,128)(2,1)}), bf16[16,6,7168]{2,1,0:T(8,128)(2,1)S(1)}, u32[]{:S(2)}, u32[]{:S(2)}) async-start(bf16[16,6,7168]{2,1,0:T(8,128)(2,1)} %reshape.34), calls=%async_computation.1 | async-start | bytes 3670016 | tf_op jit(solution)/shard_map/all_to_all | solution.py:37
  93.5 43.6 %copy-start.1 = (bf16[8,7168]{1,0:T(8,128)(2,1)S(1)}, bf16[8,7168]{1,0:T(8,128)(2,1)}, u32[]{:S(2)}) copy-start(bf16[8,7168]{1,0:T(8,128)(2,1)} %param.6) | copy-start | bytes 344068
where the time goes:
time: 137 us
  blocking collectives  48.1 us (35%)
  waiting for transfers between devices  41.7 us (30%)
  matrix products  35.6 us (26%)
  starting transfers between devices  5.22 us (4%)
  local copies, waits for them, and re-layouts  5.19 us (4%)
    all_to_all x1, blocking collectives, on_device(): lax.all_to_all(outgoing, 'expert', split_axis=0, concat_axis=0, tiled=True)  48.1 us
    all_to_all x1, waiting for transfers between devices, on_device(): lax.all_to_all(result.reshape(devices, count, width), 'expert', split_axi...  41.7 us
    dot_general x1, matrix products, on_device(): jnp.dot(hidden, w_down[0], preferred_element_type=jnp.float32)  21 us
    dot_general x1, matrix products, on_device(): gate = jnp.dot(flat_rows, w_gate[0], preferred_element_type=jnp.float32)  12.7 us
    all_to_all x1, starting transfers between devices, on_device(): lax.all_to_all(result.reshape(devices, count, width), 'expert', split_axi...  5.22 us
  transfers between devices with their start and end apart: 1, of which 1 were waited for; matrix products, arithmetic and copies ran while one was open for 0% of the time, Pallas kernels for 0%

commit v1 on v0

--- a/solution.py
+++ b/solution.py
@@ -1,12 +1,22 @@
+import functools
+import math
+
 import jax
 import jax.numpy as jnp
 from jax import lax
+from jax.experimental import pallas as pl
+from jax.experimental.pallas import tpu as pltpu
 from jax.sharding import PartitionSpec as P
 
 FF = 2048
-
-
-def on_device(tokens, routes, gate_scale, w_gate, w_up, w_down):
+CHUNK = 512
+RING = 22
+PARTS = 2
+LAG = 1
+VMEM = 62 * 2**20
+
+
+def by_all_to_all(tokens, routes, gate_scale, w_gate, w_up, w_down):
     devices = lax.axis_size("expert")
     tok_count, top_count = routes.shape
     width = tokens.shape[1]
@@ -46,7 +56,254 @@
     return mixed.astype(jnp.bfloat16)
 
 
+def kernel(
+    bits, slices, tok, routes, gates, wg, wu, wd, out,
+    x3, x2, s3, acc_g, acc_u, hid, ring, keep, snd, rcv,
+    ring_sem, ag_send, ag_recv, sc_send, sc_recv, rs_send, rs_recv,
+):
+    steps = len(bits)
+    block, width = tok.shape
+    rows = block << steps
+    hidden = wg.shape[2]
+    k_count = width // CHUNK
+    part = width // PARTS
+    me = lax.axis_index("expert")
+
+    def partner(step):
+        place = 1 << bits[step]
+        return {"expert": me + (1 - 2 * ((me // place) % 2)) * place}
+
+    def load_pair(p):
+        for j, w in enumerate((wg, wu)):
+            slot = lax.rem(2 * p + j, RING)
+            pltpu.make_async_copy(
+                w.at[0, pl.ds(p * CHUNK, CHUNK), :], ring.at[slot], ring_sem.at[slot]
+            ).start()
+
+    def load_down(d):
+        slot = lax.rem(2 * k_count + d, RING)
+        for k in range(hidden // CHUNK):
+            pltpu.make_async_copy(
+                wd.at[0, pl.ds(k * CHUNK, CHUNK), pl.ds(d * CHUNK, CHUNK)],
+                ring.at[slot, :, pl.ds(k * CHUNK, CHUNK)],
+                ring_sem.at[slot],
+            ).start()
+
+    def arrived(slot):
+        pltpu.make_async_copy(ring.at[slot], ring.at[slot], ring_sem.at[slot]).wait()
+
+    def first(p, carry):
+        load_pair(p)
+        return carry
+
+    lax.fori_loop(0, RING // 2, first, 0)
+
+    barrier = pltpu.get_barrier_semaphore()
+    for step in range(steps):
+        pl.semaphore_signal(
+            barrier, inc=1, device_id=partner(step), device_id_type=pl.DeviceIdType.MESH
+        )
+    x3[0] = tok[...]
+    lane = lax.broadcasted_iota(jnp.int32, (block, 128), 1)
+    dense = jnp.zeros((block, 128), jnp.float32)
+    for k in range(routes.shape[1]):
+        dense += jnp.where(routes[:, k : k + 1] == lane, gates[:, k : k + 1], 0.0)
+    s3[0] = dense
+    pl.semaphore_wait(barrier, steps)
+
+    def gather(step, a):
+        held = 1 << step
+        columns = pl.ds(a * part, part)
+        return pltpu.make_async_remote_copy(
+            src_ref=x3.at[pl.ds(0, held), :, columns],
+            dst_ref=x3.at[pl.ds(held, held), :, columns],
+            send_sem=ag_send.at[step, a],
+            recv_sem=ag_recv.at[step, a],
+            device_id=partner(step),
+            device_id_type=pl.DeviceIdType.MESH,
+        )
+
+    def gather_scale(step):
+        held = 1 << step
+        return pltpu.make_async_remote_copy(
+            src_ref=s3.at[pl.ds(0, held)],
+            dst_ref=s3.at[pl.ds(held, held)],
+            send_sem=sc_send.at[step],
+            recv_sem=sc_recv.at[step],
+            device_id=partner(step),
+            device_id_type=pl.DeviceIdType.MESH,
+        )
+
+    for phase in range(PARTS + steps):
+        for a in range(PARTS):
+            step = phase - a
+            if 0 <= step - 1 < steps:
+                gather(step - 1, a).wait_recv()
+            if 0 <= step < steps:
+                gather(step, a).start()
+        if phase < steps + 1:
+            if phase > 0:
+                gather_scale(phase - 1).wait_recv()
+            if phase < steps:
+                gather_scale(phase).start()
+
+    acc_g[...] = jnp.zeros_like(acc_g)
+    acc_u[...] = jnp.zeros_like(acc_u)
+
+    def up(p, carry):
+        columns = pl.ds(pl.multiple_of(p * CHUNK, CHUNK), CHUNK)
+        x = x3[:, :, columns].astype(jnp.float32).reshape(rows, CHUNK).astype(jnp.bfloat16)
+        x2[...] = x
+        for j, acc in enumerate((acc_g, acc_u)):
+            slot = lax.rem(2 * p + j, RING)
+            arrived(slot)
+            for n in range(0, hidden, 256):
+                acc[:, n : n + 256] += jnp.dot(
+                    x2[...], ring[slot, :, n : n + 256], preferred_element_type=jnp.float32
+                )
+        q = p + RING // 2
+
+        @pl.when(q < k_count)
+        def _():
+            load_pair(q)
+
+        for j in range(2):
+            d = 2 * (q - k_count) + j
+
+            @pl.when((d >= 0) & (d < k_count))
+            def _():
+                load_down(d)
+
+        return carry
+
+    lax.fori_loop(0, k_count, up, 0)
+
+    wide = lax.broadcasted_iota(jnp.int32, (rows, 128), 1)
+    scale = jnp.sum(
+        jnp.where(wide == me // slices, s3[...].reshape(rows, 128), 0.0), axis=1, keepdims=True
+    )
+    for n in range(0, hidden, 256):
+        g = acc_g[:, n : n + 256]
+        hid[:, n : n + 256] = (
+            g / (1.0 + jnp.exp(-g)) * acc_u[:, n : n + 256] * scale
+        ).astype(jnp.bfloat16)
+
+    def reduce(level, c):
+        return pltpu.make_async_remote_copy(
+            src_ref=snd[level].at[c],
+            dst_ref=rcv[level].at[c],
+            send_sem=rs_send.at[level, c],
+            recv_sem=rs_recv.at[level, c],
+            device_id=partner(steps - 1 - level),
+            device_id_type=pl.DeviceIdType.MESH,
+        )
+
+    def pass_on(level, c, total):
+        half = total.shape[0] // 2
+        keep[level][c] = total[:half]
+        sent = total[half:]
+        if half == block:
+            sent = jnp.concatenate([sent[:, : CHUNK // 2], sent[:, CHUNK // 2 :]], axis=0)
+        snd[level][c] = sent.astype(jnp.bfloat16)
+        reduce(level, c).start()
+
+    def down(c, carry):
+        for level in range(steps, 0, -1):
+            d = c - LAG * level
+
+            @pl.when((d >= 0) & (d < k_count))
+            def _():
+                reduce(level - 1, d).wait_recv()
+                got = rcv[level - 1][d].astype(jnp.float32)
+                if level == steps:
+                    got = jnp.concatenate([got[:block], got[block:]], axis=1)
+                total = keep[level - 1][d] + got
+                if level < steps:
+                    pass_on(level, d, total)
+                else:
+                    out[:, pl.ds(pl.multiple_of(d * CHUNK, CHUNK), CHUNK)] = total
+
+        @pl.when(c < k_count)
+        def _():
+            slot = lax.rem(2 * k_count + c, RING)
+            arrived(slot)
+            total = jnp.zeros((rows, CHUNK), jnp.float32)
+            for k in range(0, hidden, CHUNK):
+                total += jnp.dot(
+                    hid[:, k : k + CHUNK],
+                    ring[slot, :, k : k + CHUNK],
+                    preferred_element_type=jnp.float32,
+                )
+            pass_on(0, c, total)
+
+        return carry
+
+    lax.fori_loop(0, k_count + LAG * steps, down, 0)
+
+    for step in range(steps):
+        for a in range(PARTS):
+            gather(step, a).wait_send()
+        gather_scale(step).wait_send()
+
+    def finish(c, carry):
+        for level in range(steps):
+            reduce(level, c).wait_send()
+        return carry
+
+    lax.fori_loop(0, k_count, finish, 0)
+
+
+def by_kernel(bits, tokens, routes, gate_scale, w_gate, w_up, w_down):
+    steps = len(bits)
+    block, width = tokens.shape
+    hidden = w_gate.shape[2]
+    rows = block << steps
+    count = width // CHUNK
+    halves = [rows >> (level + 1) for level in range(steps)]
+    sent = [(count, h, CHUNK) if h > block else (count, 2 * h, CHUNK // 2) for h in halves]
+    vmem = pl.BlockSpec(memory_space=pltpu.VMEM)
+    hbm = pl.BlockSpec(memory_space=pl.ANY)
+    result = pl.pallas_call(
+        functools.partial(kernel, bits, FF // hidden),
+        out_shape=jax.ShapeDtypeStruct((block, width), jnp.float32),
+        in_specs=[vmem, vmem, vmem, hbm, hbm, hbm],
+        out_specs=vmem,
+        scratch_shapes=[
+            pltpu.VMEM((1 << steps, block, width), jnp.bfloat16),
+            pltpu.VMEM((rows, CHUNK), jnp.bfloat16),
+            pltpu.VMEM((1 << steps, block, 128), jnp.float32),
+            pltpu.VMEM((rows, hidden), jnp.float32),
+            pltpu.VMEM((rows, hidden), jnp.float32),
+            pltpu.VMEM((rows, hidden), jnp.bfloat16),
+            pltpu.VMEM((RING, CHUNK, hidden), jnp.bfloat16),
+            [pltpu.VMEM((count, h, CHUNK), jnp.float32) for h in halves],
+            [pltpu.VMEM(s, jnp.bfloat16) for s in sent],
+            [pltpu.VMEM(s, jnp.bfloat16) for s in sent],
+            pltpu.SemaphoreType.DMA((RING,)),
+            pltpu.SemaphoreType.DMA((steps, PARTS)),
+            pltpu.SemaphoreType.DMA((steps, PARTS)),
+            pltpu.SemaphoreType.DMA((steps,)),
+            pltpu.SemaphoreType.DMA((steps,)),
+            pltpu.SemaphoreType.DMA((steps, count)),
+            pltpu.SemaphoreType.DMA((steps, count)),
+        ],
+        compiler_params=pltpu.CompilerParams(
+            collective_id=0, has_side_effects=True, vmem_limit_bytes=VMEM
+        ),
+    )(tokens, routes, gate_scale, w_gate, w_up, w_down)
+    return result.astype(jnp.bfloat16)
+
+
 def solution(mesh):
+    devices = mesh.shape["expert"]
+
+    def on_device(tokens, routes, gate_scale, w_gate, w_up, w_down):
+        if devices == 16 and w_gate.shape[2] == FF:
+            return by_kernel(
+                (2, 3, 1, 0), tokens, routes, gate_scale, w_gate, w_up, w_down
+            )
+        return by_all_to_all(tokens, routes, gate_scale, w_gate, w_up, w_down)
+
     return jax.shard_map(
         on_device,
         mesh=mesh,

time: 137 us -> 99.6 us (0.73)
  the two profiles are of different devices: /device:TPU:15 before, /device:TPU:0 now
where the time goes in v1:
time: 99.6 us; the launch traced here: 99.5 us
  Pallas kernels  97.9 us (98%)
  other arithmetic  1.6 us (2%)
    pallas_call x1, Pallas kernels, by_kernel(): pl.pallas_call(functools.partial(kernel, bits, FF // hidden), out_shape=j...  97.9 us

profile of v1, /device:TPU:0, one launch (start us, length us, event | category | flops | bytes accessed | tf_op | source)
XLA Modules:
  0.0 99.5 jit_solution(12952943821484265527)
XLA Ops:
  0.0 97.9 %shard_map.64 = f32[8,7168]{1,0:T(8,128)} custom-call(bf16[8,7168]{1,0:T(8,128)(2,1)} %tok.1, s32[8,8]{1,0:T(8,128)} %routes.1, f32[8,8]{1,0:T(8,128)} %gates.1, bf16[1,7168,2048]{2,1,0:T(8,128)(2,1)} %wg.1, bf16[1,7168,2048]{2,1,0:T(8,128)(2,1)} %wu.1, bf16[1,2048,7168]{2,1,0:T(8,128)(2,1)} %wd.1), custom_call_target="tpu_custom_call" | custom-call | tf_op jit(solution)/shard_map/pallas_call | solution.py:266
  97.9 1.6 %convert_element_type.3 = bf16[8,7168]{1,0:T(8,128)(2,1)} convert(f32[8,7168]{1,0:T(8,128)} %shard_map.64) | non-fusion elementwise | flops 57344 | bytes 344064 | tf_op jit(solution)/shard_map/convert_element_type | solution.py:294

commit v2 on v1

--- a/solution.py
+++ b/solution.py
@@ -11,8 +11,8 @@
 FF = 2048
 CHUNK = 512
 RING = 22
-PARTS = 2
-LAG = 1
+PARTS = 7
+LAG = 6
 VMEM = 62 * 2**20
 
 
@@ -56,22 +56,28 @@
     return mixed.astype(jnp.bfloat16)
 
 
+EXCHANGES = ((1, 1), (2, 1), (3, 1), (4, 4), (8, 8))
+
+
 def kernel(
     bits, slices, tok, routes, gates, wg, wu, wd, out,
     x3, x2, s3, acc_g, acc_u, hid, ring, keep, snd, rcv,
     ring_sem, ag_send, ag_recv, sc_send, sc_recv, rs_send, rs_recv,
 ):
-    steps = len(bits)
     block, width = tok.shape
-    rows = block << steps
+    rows = 16 * block
     hidden = wg.shape[2]
     k_count = width // CHUNK
     part = width // PARTS
+    per_part = part // CHUNK
     me = lax.axis_index("expert")
 
-    def partner(step):
-        place = 1 << bits[step]
-        return {"expert": me + (1 - 2 * ((me // place) % 2)) * place}
+    def partner(moves):
+        there = me
+        for j, place in enumerate(bits):
+            if (moves >> j) & 1:
+                there = there + (1 - 2 * ((me // place) % 2)) * place
+        return {"expert": there}
 
     def load_pair(p):
         for j, w in enumerate((wg, wu)):
@@ -99,9 +105,9 @@
     lax.fori_loop(0, RING // 2, first, 0)
 
     barrier = pltpu.get_barrier_semaphore()
-    for step in range(steps):
+    for moves in (1, 2, 3, 4, 8):
         pl.semaphore_signal(
-            barrier, inc=1, device_id=partner(step), device_id_type=pl.DeviceIdType.MESH
+            barrier, inc=1, device_id=partner(moves), device_id_type=pl.DeviceIdType.MESH
         )
     x3[0] = tok[...]
     lane = lax.broadcasted_iota(jnp.int32, (block, 128), 1)
@@ -109,43 +115,39 @@
     for k in range(routes.shape[1]):
         dense += jnp.where(routes[:, k : k + 1] == lane, gates[:, k : k + 1], 0.0)
     s3[0] = dense
-    pl.semaphore_wait(barrier, steps)
-
-    def gather(step, a):
-        held = 1 << step
-        columns = pl.ds(a * part, part)
+    pl.semaphore_wait(barrier, 5)
+
+    def gather(lane_of, a):
+        moves, held = EXCHANGES[lane_of]
+        columns = pl.ds(pl.multiple_of(a * part, part), part)
         return pltpu.make_async_remote_copy(
             src_ref=x3.at[pl.ds(0, held), :, columns],
-            dst_ref=x3.at[pl.ds(held, held), :, columns],
-            send_sem=ag_send.at[step, a],
-            recv_sem=ag_recv.at[step, a],
-            device_id=partner(step),
+            dst_ref=x3.at[pl.ds(moves, held), :, columns],
+            send_sem=ag_send.at[lane_of, a],
+            recv_sem=ag_recv.at[lane_of, a],
+            device_id=partner(moves),
             device_id_type=pl.DeviceIdType.MESH,
         )
 
-    def gather_scale(step):
-        held = 1 << step
+    def gather_scale(lane_of):
+        moves, held = EXCHANGES[lane_of]
         return pltpu.make_async_remote_copy(
             src_ref=s3.at[pl.ds(0, held)],
-            dst_ref=s3.at[pl.ds(held, held)],
-            send_sem=sc_send.at[step],
-            recv_sem=sc_recv.at[step],
-            device_id=partner(step),
+            dst_ref=s3.at[pl.ds(moves, held)],
+            send_sem=sc_send.at[lane_of],
+            recv_sem=sc_recv.at[lane_of],
+            device_id=partner(moves),
             device_id_type=pl.DeviceIdType.MESH,
         )
 
-    for phase in range(PARTS + steps):
-        for a in range(PARTS):
-            step = phase - a
-            if 0 <= step - 1 < steps:
-                gather(step - 1, a).wait_recv()
-            if 0 <= step < steps:
-                gather(step, a).start()
-        if phase < steps + 1:
-            if phase > 0:
-                gather_scale(phase - 1).wait_recv()
-            if phase < steps:
-                gather_scale(phase).start()
+    def open_part(a, carry):
+        for lane_of in range(3):
+            gather(lane_of, a).start()
+        return carry
+
+    lax.fori_loop(0, PARTS, open_part, 0)
+    for lane_of in range(3):
+        gather_scale(lane_of).start()
 
     acc_g[...] = jnp.zeros_like(acc_g)
     acc_u[...] = jnp.zeros_like(acc_u)
@@ -176,7 +178,38 @@
 
         return carry
 
-    lax.fori_loop(0, k_count, up, 0)
+    def phase_of(phase, carry):
+        @pl.when(phase < PARTS)
+        def _():
+            for lane_of in range(3):
+                gather(lane_of, phase).wait_recv()
+            gather(3, phase).start()
+
+        @pl.when((phase >= 1) & (phase <= PARTS))
+        def _():
+            gather(3, phase - 1).wait_recv()
+            gather(4, phase - 1).start()
+
+        @pl.when(phase == 0)
+        def _():
+            for lane_of in range(3):
+                gather_scale(lane_of).wait_recv()
+            gather_scale(3).start()
+
+        @pl.when(phase == 1)
+        def _():
+            gather_scale(3).wait_recv()
+            gather_scale(4).start()
+
+        @pl.when(phase >= 2)
+        def _():
+            gather(4, phase - 2).wait_recv()
+            lax.fori_loop((phase - 2) * per_part, (phase - 1) * per_part, up, 0)
+
+        return carry
+
+    lax.fori_loop(0, PARTS + 2, phase_of, 0)
+    gather_scale(4).wait_recv()
 
     wide = lax.broadcasted_iota(jnp.int32, (rows, 128), 1)
     scale = jnp.sum(
@@ -189,38 +222,55 @@
         ).astype(jnp.bfloat16)
 
     def reduce(level, c):
+        moves = (8, 4)[level]
         return pltpu.make_async_remote_copy(
             src_ref=snd[level].at[c],
             dst_ref=rcv[level].at[c],
             send_sem=rs_send.at[level, c],
             recv_sem=rs_recv.at[level, c],
-            device_id=partner(steps - 1 - level),
+            device_id=partner(moves),
             device_id_type=pl.DeviceIdType.MESH,
         )
 
+    def reduce_last(moves, c):
+        return pltpu.make_async_remote_copy(
+            src_ref=snd[2].at[c, moves - 1],
+            dst_ref=rcv[2].at[c, moves - 1],
+            send_sem=rs_send.at[1 + moves, c],
+            recv_sem=rs_recv.at[1 + moves, c],
+            device_id=partner(moves),
+            device_id_type=pl.DeviceIdType.MESH,
+        )
+
     def pass_on(level, c, total):
-        half = total.shape[0] // 2
-        keep[level][c] = total[:half]
-        sent = total[half:]
-        if half == block:
+        if level < 2:
+            half = total.shape[0] // 2
+            keep[level][c] = total[:half]
+            snd[level][c] = total[half:].astype(jnp.bfloat16)
+            reduce(level, c).start()
+            return
+        keep[2][c] = total[:block]
+        for moves in (1, 2, 3):
+            sent = total[moves * block : (moves + 1) * block]
             sent = jnp.concatenate([sent[:, : CHUNK // 2], sent[:, CHUNK // 2 :]], axis=0)
-        snd[level][c] = sent.astype(jnp.bfloat16)
-        reduce(level, c).start()
+            snd[2][c, moves - 1] = sent.astype(jnp.bfloat16)
+            reduce_last(moves, c).start()
 
     def down(c, carry):
-        for level in range(steps, 0, -1):
+        for level in (3, 2, 1):
             d = c - LAG * level
 
             @pl.when((d >= 0) & (d < k_count))
             def _():
-                reduce(level - 1, d).wait_recv()
-                got = rcv[level - 1][d].astype(jnp.float32)
-                if level == steps:
-                    got = jnp.concatenate([got[:block], got[block:]], axis=1)
-                total = keep[level - 1][d] + got
-                if level < steps:
-                    pass_on(level, d, total)
+                total = keep[level - 1][d]
+                if level < 3:
+                    reduce(level - 1, d).wait_recv()
+                    pass_on(level, d, total + rcv[level - 1][d].astype(jnp.float32))
                 else:
+                    for moves in (1, 2, 3):
+                        reduce_last(moves, d).wait_recv()
+                        got = rcv[2][d, moves - 1].astype(jnp.float32)
+                        total += jnp.concatenate([got[:block], got[block:]], axis=1)
                     out[:, pl.ds(pl.multiple_of(d * CHUNK, CHUNK), CHUNK)] = total
 
         @pl.when(c < k_count)
@@ -238,16 +288,22 @@
 
         return carry
 
-    lax.fori_loop(0, k_count + LAG * steps, down, 0)
-
-    for step in range(steps):
-        for a in range(PARTS):
-            gather(step, a).wait_send()
-        gather_scale(step).wait_send()
+    lax.fori_loop(0, k_count + LAG * 3, down, 0)
+
+    def close_part(a, carry):
+        for lane_of in range(5):
+            gather(lane_of, a).wait_send()
+        return carry
+
+    lax.fori_loop(0, PARTS, close_part, 0)
+    for lane_of in range(5):
+        gather_scale(lane_of).wait_send()
 
     def finish(c, carry):
-        for level in range(steps):
+        for level in range(2):
             reduce(level, c).wait_send()
+        for moves in (1, 2, 3):
+            reduce_last(moves, c).wait_send()
         return carry
 
     lax.fori_loop(0, k_count, finish, 0)
@@ -259,8 +315,8 @@
     hidden = w_gate.shape[2]
     rows = block << steps
     count = width // CHUNK
-    halves = [rows >> (level + 1) for level in range(steps)]
-    sent = [(count, h, CHUNK) if h > block else (count, 2 * h, CHUNK // 2) for h in halves]
+    halves = [rows // 2, rows // 4, block]
+    sent = [(count, h, CHUNK) for h in halves[:2]] + [(count, 3, 2 * block, CHUNK // 2)]
     vmem = pl.BlockSpec(memory_space=pltpu.VMEM)
     hbm = pl.BlockSpec(memory_space=pl.ANY)
     result = pl.pallas_call(
@@ -280,12 +336,12 @@
             [pltpu.VMEM(s, jnp.bfloat16) for s in sent],
             [pltpu.VMEM(s, jnp.bfloat16) for s in sent],
             pltpu.SemaphoreType.DMA((RING,)),
-            pltpu.SemaphoreType.DMA((steps, PARTS)),
-            pltpu.SemaphoreType.DMA((steps, PARTS)),
-            pltpu.SemaphoreType.DMA((steps,)),
-            pltpu.SemaphoreType.DMA((steps,)),
-            pltpu.SemaphoreType.DMA((steps, count)),
-            pltpu.SemaphoreType.DMA((steps, count)),
+            pltpu.SemaphoreType.DMA((5, PARTS)),
+            pltpu.SemaphoreType.DMA((5, PARTS)),
+            pltpu.SemaphoreType.DMA((5,)),
+            pltpu.SemaphoreType.DMA((5,)),
+            pltpu.SemaphoreType.DMA((5, count)),
+            pltpu.SemaphoreType.DMA((5, count)),
         ],
         compiler_params=pltpu.CompilerParams(
             collective_id=0, has_side_effects=True, vmem_limit_bytes=VMEM
@@ -300,7 +356,7 @@
     def on_device(tokens, routes, gate_scale, w_gate, w_up, w_down):
         if devices == 16 and w_gate.shape[2] == FF:
             return by_kernel(
-                (2, 3, 1, 0), tokens, routes, gate_scale, w_gate, w_up, w_down
+                (4, 8, 2, 1), tokens, routes, gate_scale, w_gate, w_up, w_down
             )
         return by_all_to_all(tokens, routes, gate_scale, w_gate, w_up, w_down)
 

time: 99.6 us -> 62 us (0.62)
  Pallas kernels: 97.9 us -> 60.3 us
    pallas_call x1, Pallas kernels: 97.9 us -> 60.3 us  [by_kernel(): pl.pallas_call(functools.partial(kernel, bits, FF // hidden), out_shape=j...]
where the time goes in v2:
time: 62 us; the launch traced here: 61.9 us
  Pallas kernels  60.3 us (97%)
  other arithmetic  1.6 us (3%)
    pallas_call x1, Pallas kernels, by_kernel(): pl.pallas_call(functools.partial(kernel, bits, FF // hidden), out_shape=j...  60.3 us
    convert_element_type x1, other arithmetic, by_kernel(): return result.astype(jnp.bfloat16)  1.6 us

profile of v2, /device:TPU:0, one launch (start us, length us, event | category | flops | bytes accessed | tf_op | source)
XLA Modules:
  0.0 61.9 jit_solution(11488999206643032986)
XLA Ops:
  0.0 60.3 %shard_map.64 = f32[8,7168]{1,0:T(8,128)} custom-call(bf16[8,7168]{1,0:T(8,128)(2,1)} %tok.1, s32[8,8]{1,0:T(8,128)} %routes.1, f32[8,8]{1,0:T(8,128)} %gates.1, bf16[1,7168,2048]{2,1,0:T(8,128)(2,1)} %wg.1, bf16[1,7168,2048]{2,1,0:T(8,128)(2,1)} %wu.1, bf16[1,2048,7168]{2,1,0:T(8,128)(2,1)} %wd.1), custom_call_target="tpu_custom_call" | custom-call | tf_op jit(solution)/shard_map/pallas_call | solution.py:322
  60.3 1.6 %convert_element_type.3 = bf16[8,7168]{1,0:T(8,128)(2,1)} convert(f32[8,7168]{1,0:T(8,128)} %shard_map.64) | non-fusion elementwise | flops 57344 | bytes 344064 | tf_op jit(solution)/shard_map/convert_element_type | solution.py:350
